TPU v7x, 32 devices: a whole 2x2x4 slice. The times are simulated.
32 devices in a mesh: tm: 8 (over y, x, core), ctr: 4 (over z).
Axes of the slice: x: 2, y: 2, z: 4, core: 2. Of those that a mesh axis runs over, the one named last changes fastest.
Arguments:
- target: float32 [64, 262144], P('ctr', 'tm'), may hold values from -6 to 6
- sparse: float32 [64, 262144], P('ctr', 'tm'), may hold values from -6 to 6
- kernel: float32 [64, 262144], P('ctr', 'tm'), may hold values from -0.03314563 to 0.03314563
- penalty: float32 [64], P('ctr'), may hold values from 0.5 to 5
Outputs:
- updated: float32 [64, 262144], P('ctr', 'tm')
- residual: float32 [64, 262144], P('ctr', 'tm')
- objective: float32 [], replicated
All inputs are finite; a program needn't handle non-finite values.
Results may differ from a plain program's by a relative error of at most 0.0003.
Values sent between devices are 32-bit elements; how exact they have to be, the bound alone decides.
A program may use at most 128 MiB of HBM per device.

v0:
```python
import math

import jax
import jax.numpy as jnp
from jax import lax
from jax.sharding import PartitionSpec as P

FACTOR = 512
LENGTH = 262144


HIGHEST = lax.Precision.HIGHEST


def tables(row_index, column_index, modulus):
    product = row_index[:, None] * column_index[None, :] % modulus
    angle = product.astype(jnp.float32) * (2.0 * math.pi / modulus)
    return (jnp.cos(angle), jnp.sin(angle))


def left_product(table, matrix):
    return jnp.dot(table, matrix, precision=HIGHEST, preferred_element_type=jnp.float32)


def turn_forward(real_part, imag_part, twist_cos, twist_sin):
    return (
        real_part * twist_cos + imag_part * twist_sin,
        imag_part * twist_cos - real_part * twist_sin,
    )


def turn_inverse(real_part, imag_part, twist_cos, twist_sin):
    return (
        real_part * twist_cos - imag_part * twist_sin,
        real_part * twist_sin + imag_part * twist_cos,
    )


def spectral_step(kernel_even, kernel_odd, sparse_even, sparse_odd, target_even, target_odd):
    resid_even = target_even - (kernel_even * sparse_even - kernel_odd * sparse_odd)
    resid_odd = target_odd - (kernel_even * sparse_odd + kernel_odd * sparse_even)
    grad_even = kernel_even * resid_even + kernel_odd * resid_odd
    grad_odd = kernel_even * resid_odd - kernel_odd * resid_even
    return (resid_even, resid_odd, grad_even, grad_odd)


def shrink(sparse, gradient, step_size, penalty):
    shifted = sparse + step_size[:, None] * gradient
    return jnp.sign(shifted) * jnp.maximum(jnp.abs(shifted) - (step_size * penalty)[:, None], 0.0)


def regroup_rows(matrix, parts, width, groups, counters):
    shaped = matrix.reshape(parts, width, groups, counters, width)
    return shaped.transpose(0, 4, 2, 3, 1).reshape(parts, width, groups * counters * width)


def shards(target, sparse, kernel, penalty):
    time_parts = lax.axis_size("tm")
    block_number = lax.axis_index("tm")
    counters, time_span = sparse.shape
    index_ramp = jnp.arange(FACTOR, dtype=jnp.int32)
    cos_table, sin_table = tables(index_ramp, index_ramp, FACTOR)
    block_width = FACTOR // time_parts
    span = counters * block_width
    stacked = jnp.stack((sparse, target, kernel), 0).reshape(
        3, counters, block_width, time_parts, block_width
    )
    outgoing = stacked.transpose(2, 3, 0, 1, 4).reshape(block_width, time_parts, 3 * span)
    columns = lax.all_to_all(outgoing, "tm", split_axis=1, concat_axis=0, tiled=True).reshape(
        FACTOR, 3 * span
    )
    left_real = left_product(cos_table, columns)
    left_imag = -left_product(sin_table, columns)
    forward_cols = block_number * block_width + jnp.arange(3 * span, dtype=jnp.int32) % block_width
    twist_cos, twist_sin = tables(index_ramp, forward_cols, LENGTH)
    turned_real, turned_imag = turn_forward(left_real, left_imag, twist_cos, twist_sin)
    turned_real, turned_imag = (
        lax.all_to_all(
            regroup_rows(turned_real, time_parts, block_width, 3, counters),
            "tm",
            split_axis=0,
            concat_axis=1,
            tiled=True,
        ),
        lax.all_to_all(
            regroup_rows(turned_imag, time_parts, block_width, 3, counters),
            "tm",
            split_axis=0,
            concat_axis=1,
            tiled=True,
        ),
    )
    turned_real = turned_real.reshape(FACTOR, 3 * span)
    turned_imag = turned_imag.reshape(FACTOR, 3 * span)
    even_part = left_product(cos_table, turned_real) + left_product(sin_table, turned_imag)
    odd_part = left_product(sin_table, turned_real) - left_product(cos_table, turned_imag)
    kernel_even = even_part[:, 2 * span :]
    kernel_odd = odd_part[:, 2 * span :]
    power = (kernel_even * kernel_even + kernel_odd * kernel_odd).reshape(
        FACTOR, counters, block_width
    )
    local_peak = jnp.max(power, axis=(0, 2))
    peak_power = lax.pmax(local_peak, "tm")
    resid_even, resid_odd, grad_even, grad_odd = spectral_step(
        kernel_even,
        kernel_odd,
        even_part[:, :span],
        odd_part[:, :span],
        even_part[:, span : 2 * span],
        odd_part[:, span : 2 * span],
    )
    both_even = jnp.concatenate((resid_even, grad_even), 1)
    both_odd = jnp.concatenate((resid_odd, grad_odd), 1)
    first_real = left_product(cos_table, both_even) + left_product(sin_table, both_odd)
    first_imag = left_product(sin_table, both_even) - left_product(cos_table, both_odd)
    inverse_cols = block_number * block_width + jnp.arange(2 * span, dtype=jnp.int32) % block_width
    back_cos, back_sin = tables(index_ramp, inverse_cols, LENGTH)
    turned_real, turned_imag = turn_inverse(first_real, first_imag, back_cos, back_sin)
    turned_real, turned_imag = (
        lax.all_to_all(
            regroup_rows(turned_real, time_parts, block_width, 2, counters),
            "tm",
            split_axis=0,
            concat_axis=1,
            tiled=True,
        ),
        lax.all_to_all(
            regroup_rows(turned_imag, time_parts, block_width, 2, counters),
            "tm",
            split_axis=0,
            concat_axis=1,
            tiled=True,
        ),
    )
    turned_real = turned_real.reshape(FACTOR, 2 * span)
    turned_imag = turned_imag.reshape(FACTOR, 2 * span)
    series = (left_product(cos_table, turned_real) - left_product(sin_table, turned_imag)) / LENGTH
    series = lax.all_to_all(
        series.reshape(time_parts, block_width * 2 * span),
        "tm",
        split_axis=0,
        concat_axis=0,
        tiled=True,
    )
    series = series.reshape(time_parts, block_width, 2, counters, block_width)
    series = series.transpose(2, 3, 1, 0, 4).reshape(2, counters, time_span)
    residual = series[0]
    updated = shrink(sparse, series[1], 1.0 / peak_power, penalty)
    partial_value = 0.5 * jnp.sum(residual * residual) + jnp.sum(penalty[:, None] * jnp.abs(sparse))
    objective_total = lax.psum(partial_value, ("tm", "ctr"))
    objective = objective_total / (LENGTH * counters * lax.axis_size("ctr"))
    return (updated, residual, objective)


def solution(mesh):
    placed = (P("ctr", "tm"), P("ctr", "tm"), P("ctr", "tm"), P("ctr"))
    return jax.shard_map(
        shards,
        mesh=mesh,
        in_specs=placed,
        out_specs=(P("ctr", "tm"), P("ctr", "tm"), P()),
        check_vma=False,
    )
```

profile of v0, /device:TPU:0, one launch (start us, length us, event | category | flops | bytes accessed | tf_op | source)
XLA Modules:
  0.0 798.8 jit_solution(8746496437750038637)
XLA Ops:
  31.1 9.7 %maximum_bitcast_fusion = f32[64,8,3,16,64]{4,3,2,1,0:T(8,128)} fusion(f32[1,16,64,8,64]{4,1,0,3,2:T(8,128)} %copy.30, f32[1,16,64,8,64]{4,1,0,3,2:T(8,128)S(1)} %copy-done.1, f32[1,16,64,8,64]{4,1,0,3,2:T(8,128)} %copy.28), kind=kLoop, calls=%fused_computation | loop fusion | flops 3145728 | bytes 12582912 | tf_op jit(solution)/shard_map/transpose | solution.py:68
  40.8 10.9 %reshape.110 = f32[64,8,3072]{2,1,0:T(8,128)} reshape(f32[64,8,3,16,64]{4,3,2,1,0:T(8,128)} %maximum_bitcast_fusion) | data formatting | bytes 12582912 | tf_op jit(solution)/shard_map/reshape | solution.py:68
  51.6 9.1 %copy.31 = f32[64,8,3072]{2,0,1:T(8,128)} copy(f32[64,8,3072]{2,1,0:T(8,128)} %reshape.110) | data formatting | bytes 12582912 | tf_op jit(solution)/shard_map/reshape | solution.py:68
  69.7 68.0 %all-to-all-done = f32[64,8,3072]{2,0,1:T(8,128)} async-done(((f32[64,8,3072]{2,0,1:T(8,128)}), f32[64,8,3072]{2,0,1:T(8,128)}, u32[]{:S(2)}, u32[]{:S(2)}) %all-to-all-start) | async-done | bytes 6291488 | tf_op jit(solution)/shard_map/all_to_all | solution.py:69
  137.7 26.6 %fusion.45 = f32[512,3072]{1,0:T(8,128)S(1)} fusion(f32[512,3072]{1,0:T(8,128)} %bitcast.3), kind=kOutput, calls=%fused_computation.61 | convolution fusion | flops 9667346432 | bytes 12582912 | tf_op jit(solution)/shard_map/dot_general | solution.py:22
  164.4 38.2 %multiply_subtract_fusion = (f32[512,3072]{1,0:T(8,128)}, f32[512,3072]{1,0:T(8,128)}) fusion(f32[512,3072]{1,0:T(8,128)S(1)} %fusion.45, s32[3072]{0:T(1024)S(1)} %fusion.47, f32[512,3072]{1,0:T(8,128)} %bitcast.3, f32[512,512]{1,0:T(8,128)S(1)} %fusion.38.clone.4), kind=kOutput, calls=%fused_computation.10 | convolution fusion | flops 9696706560 | bytes 26226688 | tf_op jit(solution)/shard_map/dot_general | solution.py:22
  202.5 10.0 %reshape.112 = f32[8,64,3,16,64]{4,3,2,1,0:T(8,128)} reshape(f32[512,3072]{1,0:T(8,128)} %get-tuple-element.9) | data formatting | bytes 12582912 | tf_op jit(solution)/shard_map/reshape | solution.py:53
  212.5 13.9 %copy.32 = f32[8,64,3,16,64]{1,3,2,4,0:T(8,128)} copy(f32[8,64,3,16,64]{4,3,2,1,0:T(8,128)} %reshape.112) | data formatting | bytes 12582912 | tf_op jit(solution)/shard_map/reshape | solution.py:53
  226.4 10.6 %reshape.113 = f32[8,64,3072]{2,1,0:T(8,128)} reshape(f32[8,64,3,16,64]{4,3,2,1,0:T(8,128)} %bitcast.41) | data formatting | bytes 12582912 | tf_op jit(solution)/shard_map/reshape | solution.py:54
  241.8 10.0 %reshape.115 = f32[8,64,3,16,64]{4,3,2,1,0:T(8,128)} reshape(f32[512,3072]{1,0:T(8,128)} %get-tuple-element.8) | data formatting | bytes 12582912 | tf_op jit(solution)/shard_map/reshape | solution.py:53
  251.8 13.9 %copy.33 = f32[8,64,3,16,64]{1,3,2,4,0:T(8,128)} copy(f32[8,64,3,16,64]{4,3,2,1,0:T(8,128)} %reshape.115) | data formatting | bytes 12582912 | tf_op jit(solution)/shard_map/reshape | solution.py:53
  265.7 10.6 %reshape.116 = f32[8,64,3072]{2,1,0:T(8,128)} reshape(f32[8,64,3,16,64]{4,3,2,1,0:T(8,128)} %bitcast.42) | data formatting | bytes 12582912 | tf_op jit(solution)/shard_map/reshape | solution.py:54
  276.3 37.1 %all-to-all-done.1 = f32[8,64,3072]{2,1,0:T(8,128)} async-done(((f32[8,64,3072]{2,1,0:T(8,128)}), f32[8,64,3072]{2,1,0:T(8,128)}, u32[]{:S(2)}, u32[]{:S(2)}) %all-to-all-start.1) | async-done | bytes 6291488 | tf_op jit(solution)/shard_map/all_to_all | solution.py:78
  322.4 19.2 %fusion.42 = f32[512,3072]{1,0:T(8,128)} fusion(f32[512,3072]{1,0:T(8,128)} %bitcast.7), kind=kOutput, calls=%fused_computation.60 | convolution fusion | flops 9667346432 | bytes 12582912 | tf_op jit(solution)/shard_map/dot_general | solution.py:22
  341.6 19.3 %fusion.35 = f32[512,3072]{1,0:T(8,128)} fusion(f32[512,3072]{1,0:T(8,128)} %bitcast.7), kind=kOutput, calls=%fused_computation.58 | convolution fusion | flops 9667346432 | bytes 12582912 | tf_op jit(solution)/shard_map/dot_general | solution.py:22
  360.9 29.3 %all-to-all-done.2 = f32[8,64,3072]{2,1,0:T(8,128)} async-done(((f32[8,64,3072]{2,1,0:T(8,128)}), f32[8,64,3072]{2,1,0:T(8,128)}, u32[]{:S(2)}, u32[]{:S(2)}) %all-to-all-start.2) | async-done | bytes 6291488 | tf_op jit(solution)/shard_map/all_to_all | solution.py:85
  390.2 19.6 %convolution_subtract_fusion = f32[512,3072]{1,0:T(8,128)S(1)} fusion(f32[512,3072]{1,0:T(8,128)} %fusion.42, f32[512,3072]{1,0:T(8,128)} %bitcast.9), kind=kOutput, calls=%fused_computation.15 | convolution fusion | flops 9668919296 | bytes 18874368 | tf_op jit(solution)/shard_map/dot_general | solution.py:22
  409.8 17.5 %convolution_add_fusion = f32[512,3072]{1,0:T(8,128)S(1)} fusion(f32[512,3072]{1,0:T(8,128)S(1)} %copy-done, f32[512,3072]{1,0:T(8,128)} %bitcast.9), kind=kOutput, calls=%fused_computation.16 | convolution fusion | flops 9668919296 | bytes 18874368 | tf_op jit(solution)/shard_map/dot_general | solution.py:22
  429.9 10.9 %fusion.12 = f32[512,2048]{1,0:T(8,128)S(1)} fusion(f32[512,1024]{1,0:T(8,128)S(1)} %multiply_subtract_fusion.2, f32[512,1024]{1,0:T(8,128)S(1)} %get-tuple-element.6), kind=kOutput, calls=%fused_computation.29 | convolution fusion | flops 6447169536 | bytes 8388608 | tf_op jit(solution)/shard_map/dot_general | solution.py:22
  440.8 11.3 %fusion.13 = f32[512,2048]{1,0:T(8,128)S(1)} fusion(f32[512,1024]{1,0:T(8,128)S(1)} %multiply_subtract_fusion.2, f32[512,1024]{1,0:T(8,128)S(1)} %get-tuple-element.6), kind=kOutput, calls=%fused_computation.30 | convolution fusion | flops 6447169536 | bytes 8388608 | tf_op jit(solution)/shard_map/dot_general | solution.py:22
  452.2 11.1 %fusion.16 = f32[512,2048]{1,0:T(8,128)S(1)} fusion(f32[512,2048]{1,0:T(8,128)S(1)} %fusion.13, f32[512,1024]{1,0:T(8,128)S(1)} %get-tuple-element.5, f32[512,1024]{1,0:T(8,128)S(1)} %get-tuple-element.7), kind=kOutput, calls=%fused_computation.33 | convolution fusion | flops 6448218112 | bytes 12582912 | tf_op jit(solution)/shard_map/dot_general | solution.py:22
  463.3 25.2 %multiply_add_fusion.1 = (f32[512,2048]{1,0:T(8,128)}, f32[512,2048]{1,0:T(8,128)}) fusion(f32[512,2048]{1,0:T(8,128)S(1)} %fusion.16, s32[2048]{0:T(1024)S(1)} %fusion.51, f32[512,2048]{1,0:T(8,128)S(1)} %fusion.12, f32[512,1024]{1,0:T(8,128)S(1)} %get-tuple-element.5, f32[512,1024]{1,0:T(8,128)S(1)} %get-tuple-element.7, f32[512,512]{1,0:T(8,128)S(1)} %fusion.40.clone.5), kind=kOutput, calls=%fused_computation.24 | convolution fusion | flops 6465519616 | bytes 22028288 | tf_op jit(solution)/shard_map/dot_general | solution.py:22
  496.3 10.3 %copy.34 = f32[8,64,2,16,64]{1,3,2,4,0:T(8,128)} copy(f32[8,64,2,16,64]{4,3,2,1,0:T(8,128)} %reshape.118) | data formatting | bytes 8388608 | tf_op jit(solution)/shard_map/reshape | solution.py:53
  526.8 10.3 %copy.35 = f32[8,64,2,16,64]{1,3,2,4,0:T(8,128)} copy(f32[8,64,2,16,64]{4,3,2,1,0:T(8,128)} %reshape.121) | data formatting | bytes 8388608 | tf_op jit(solution)/shard_map/reshape | solution.py:53
  544.9 23.2 %all-to-all-done.3 = f32[8,64,2048]{2,1,0:T(8,128)} async-done(((f32[8,64,2048]{2,1,0:T(8,128)}), f32[8,64,2048]{2,1,0:T(8,128)}, u32[]{:S(2)}, u32[]{:S(2)}) %all-to-all-start.3) | async-done | bytes 4194336 | tf_op jit(solution)/shard_map/all_to_all | solution.py:120
  572.9 14.7 %fusion.30 = f32[512,2048]{1,0:T(8,128)} fusion(f32[512,2048]{1,0:T(8,128)} %bitcast.11), kind=kOutput, calls=%fused_computation.57 | convolution fusion | flops 6446120960 | bytes 8388608 | tf_op jit(solution)/shard_map/dot_general | solution.py:22
  587.6 34.4 %all-to-all-done.4 = f32[8,64,2048]{2,1,0:T(8,128)} async-done(((f32[8,64,2048]{2,1,0:T(8,128)}), f32[8,64,2048]{2,1,0:T(8,128)}, u32[]{:S(2)}, u32[]{:S(2)}) %all-to-all-start.4) | async-done | bytes 4194336 | tf_op jit(solution)/shard_map/all_to_all | solution.py:127
  622.0 15.7 %subtract_multiply_fusion = f32[512,2048]{1,0:T(8,128)} fusion(f32[512,2048]{1,0:T(8,128)} %fusion.30, f32[512,2048]{1,0:T(8,128)} %bitcast.13), kind=kOutput, calls=%fused_computation.23 | convolution fusion | flops 6448218112 | bytes 12582912 | tf_op jit(solution)/shard_map/dot_general | solution.py:22
  637.7 8.8 %all_to_all.54 = f32[8,1,131072]{2,1,0:T(1,128)} reshape(f32[512,2048]{1,0:T(8,128)} %subtract_multiply_fusion) | data formatting | bytes 8388608 | tf_op jit(solution)/shard_map/all_to_all | solution.py:138
  651.4 55.3 %pmax.7 = f32[16]{0:T(128)S(1)} all-reduce(f32[16]{0:T(128)S(1)} %reduce_max.18), channel_id=1, replica_groups=mesh['tm'=8,'ctr'=4] {'tm'}, use_global_device_ids=true, to_apply=%region_2.3 | all-reduce | flops 16 | bytes 128 | tf_op jit(solution)/shard_map/pmax | solution.py:103
  706.7 13.0 %reduce.3 = f32[8,131072]{1,0:T(8,128)} reduce(f32[8,1,131072]{2,1,0:T(1,128)} %all-to-all-done.5, f32[]{:T(128)} %constant.87), dimensions={1}, to_apply=%all_to_all.53.reduce_sub_computation | reduce | bytes 8388612 | tf_op jit(solution)/shard_map/all_to_all | solution.py:138
  756.5 40.3 %psum.7 = f32[]{:T(128)} all-reduce(f32[]{:T(128)S(6)} %add.126), channel_id=1, replica_groups=mesh['tm'=8,'ctr'=4] {'tm','ctr'}, use_global_device_ids=true, to_apply=%region_5.6 | all-reduce | flops 1 | bytes 8 | tf_op jit(solution)/shard_map/psum | solution.py:150
  (45 shorter events, 136.7 us)
Async XLA Ops:
  4.9 6.7 copy-start.4
  14.6 6.7 copy-start.2
  24.4 6.7 copy-start.1
  60.7 77.0 %all-to-all-start = ((f32[64,8,3072]{2,0,1:T(8,128)}), f32[64,8,3072]{2,0,1:T(8,128)}, u32[]{:S(2)}, u32[]{:S(2)}) async-start(f32[64,8,3072]{2,0,1:T(8,128)} %copy.31), calls=%async_computation | async-start | bytes 12582912 | tf_op jit(solution)/shard_map/all_to_all | solution.py:69
  237.0 76.4 %all-to-all-start.1 = ((f32[8,64,3072]{2,1,0:T(8,128)}), f32[8,64,3072]{2,1,0:T(8,128)}, u32[]{:S(2)}, u32[]{:S(2)}) async-start(f32[8,64,3072]{2,1,0:T(8,128)} %reshape.113), calls=%async_computation.1 | async-start | bytes 12582912 | tf_op jit(solution)/shard_map/all_to_all | solution.py:78
  313.4 76.8 %all-to-all-start.2 = ((f32[8,64,3072]{2,1,0:T(8,128)}), f32[8,64,3072]{2,1,0:T(8,128)}, u32[]{:S(2)}, u32[]{:S(2)}) async-start(f32[8,64,3072]{2,1,0:T(8,128)} %reshape.116), calls=%async_computation.2 | async-start | bytes 12582912 | tf_op jit(solution)/shard_map/all_to_all | solution.py:85
  390.2 19.6 %copy-start = (f32[512,3072]{1,0:T(8,128)S(1)}, f32[512,3072]{1,0:T(8,128)}, u32[]{:S(2)}) copy-start(f32[512,3072]{1,0:T(8,128)} %fusion.35) | copy-start | bytes 18874372
  514.4 53.7 %all-to-all-start.3 = ((f32[8,64,2048]{2,1,0:T(8,128)}), f32[8,64,2048]{2,1,0:T(8,128)}, u32[]{:S(2)}, u32[]{:S(2)}) async-start(f32[8,64,2048]{2,1,0:T(8,128)} %reshape.119), calls=%async_computation.3 | async-start | bytes 8388608 | tf_op jit(solution)/shard_map/all_to_all | solution.py:120
  568.1 53.9 %all-to-all-start.4 = ((f32[8,64,2048]{2,1,0:T(8,128)}), f32[8,64,2048]{2,1,0:T(8,128)}, u32[]{:S(2)}, u32[]{:S(2)}) async-start(f32[8,64,2048]{2,1,0:T(8,128)} %reshape.122), calls=%async_computation.4 | async-start | bytes 8388608 | tf_op jit(solution)/shard_map/all_to_all | solution.py:127
  646.5 60.1 %copy-start.5 = (f32[16]{0:T(128)S(1)}, f32[16]{0:T(128)}, u32[]{:S(2)}) copy-start(f32[16]{0:T(128)} %param.7) | copy-start | bytes 196
  646.5 60.2 %all-to-all-start.5 = ((f32[8,1,131072]{2,1,0:T(1,128)}), f32[8,1,131072]{2,1,0:T(1,128)}, u32[]{:S(2)}, u32[]{:S(2)}) async-start(f32[8,1,131072]{2,1,0:T(1,128)} %all_to_all.54), calls=%async_computation.5 | async-start | bytes 8388608 | tf_op jit(solution)/shard_map/all_to_all | solution.py:138
  742.5 4.8 copy-start.3
where the time goes:
time: 811 us; the launch traced here: 799 us
  matrix products  229 us (28%)
  local copies, waits for them, and re-layouts  206 us (25%)
  waiting for transfers between devices  192 us (24%)
  blocking collectives  95.6 us (12%)
  other arithmetic  43.1 us (5%)
  starting transfers between devices  29.1 us (4%)
    dot_general x12, matrix products, left_product(): jnp.dot(table, matrix, precision=HIGHEST, preferred_element_type=jnp.floa...  229 us
    reshape x8, local copies, waits for them, and re-layouts, regroup_rows(): shaped = matrix.reshape(parts, width, groups, counters, width)  84 us
    all_to_all x1, waiting for transfers between devices, shards(): lax.all_to_all(outgoing, 'tm', split_axis=1, concat_axis=0, tiled=True)  68 us
    pmax x1, blocking collectives, shards(): peak_power = lax.pmax(local_peak, 'tm')  55.3 us
    psum x1, blocking collectives, shards(): objective_total = lax.psum(partial_value, ('tm', 'ctr'))  40.3 us
    all_to_all x1, waiting for transfers between devices, shards(): lax.all_to_all(regroup_rows(turned_real, time_parts, block_width, 3, coun...  37.1 us
    reshape x4, local copies, waits for them, and re-layouts, regroup_rows(): shaped.transpose(0, 4, 2, 3, 1)  36.9 us
    all_to_all x1, waiting for transfers between devices, shards(): lax.all_to_all(regroup_rows(turned_imag, time_parts, block_width, 2, coun...  34.4 us
  transfers between devices with their start and end apart: 6, of which 5 were waited for; matrix products, arithmetic and copies ran while one was open for 15% of the time, Pallas kernels for 0%

commit v1 on v0

v1 whole, which is shorter than its diff:
```python
import functools

import jax
import jax.numpy as jnp
import ml_dtypes
import numpy as np
from jax import lax
from jax.experimental import pallas as pl
from jax.experimental.pallas import tpu as pltpu
from jax.sharding import PartitionSpec as P

FACTOR = 512
HALF = FACTOR // 2
ROWS = HALF + 16
TILE = 256

KERNEL, SPARSE, TARGET = 0, 1, 2


def split_table(table):
    high = table.astype(ml_dtypes.bfloat16)
    low = (table - high.astype(np.float64)).astype(ml_dtypes.bfloat16)
    return np.stack((high, low))


def make_tables():
    length = FACTOR * FACTOR
    ramp = np.arange(FACTOR)
    angle = (ramp[:, None] * ramp[None, :] % FACTOR) * (2.0 * np.pi / FACTOR)
    cos_table, sin_table = np.cos(angle), np.sin(angle)
    first = np.concatenate((cos_table[:ROWS], -sin_table[:ROWS]), 0)
    second = np.concatenate(
        (
            np.concatenate((cos_table, sin_table), 1),
            np.concatenate((sin_table, -cos_table), 1),
        ),
        0,
    )
    cos_half = 2.0 * cos_table[:, :HALF]
    cos_half[:, 0] = 1.0
    sin_half = -2.0 * sin_table[:, :HALF]
    sin_half[:, 0] = cos_table[:, HALF]
    last = np.concatenate((cos_half, sin_half), 1) / length
    twist = (np.arange(ROWS)[:, None] * ramp[None, :]) * (2.0 * np.pi / length)
    turn = np.stack((np.cos(twist), np.sin(twist))).astype(np.float32)
    return split_table(first), split_table(second), split_table(last), turn


def halves(value):
    high = value.astype(jnp.bfloat16)
    low = (value - high.astype(jnp.float32)).astype(jnp.bfloat16)
    return high, low


def dot3(left, right):
    (left_high, left_low), (right_high, right_low) = left, right
    dot = functools.partial(jnp.dot, preferred_element_type=jnp.float32)
    return dot(left_high, right_high) + (dot(left_low, right_high) + dot(left_high, right_low))


def body(
    parts,
    each,
    block_rows,
    kernel_in,
    sparse_in,
    target_in,
    penalty_in,
    first_in,
    second_in,
    last_in,
    turn_in,
    updated_out,
    residual_out,
    terms_out,
    held,
    spectra,
    mid_high,
    mid_low,
    back_high,
    back_low,
    done,
    first,
    second,
    last,
    turn,
    table_sem,
    in_send,
    in_recv,
    out_send,
    out_recv,
):
    me = lax.axis_index("tm")
    my_rows = pl.ds(pl.multiple_of(me * block_rows, block_rows), block_rows)
    inputs = (kernel_in, sparse_in, target_in)
    outputs = (residual_out, updated_out)

    def peer_rows(peer):
        return pl.ds(pl.multiple_of(peer * block_rows, block_rows), block_rows)

    def send_in(series, j, step):
        peer = lax.rem(me + step, parts)
        return pltpu.make_async_remote_copy(
            src_ref=inputs[series].at[peer * each + j],
            dst_ref=held.at[series, j, my_rows],
            send_sem=in_send.at[series, j, step],
            recv_sem=in_recv.at[series, j, step],
            device_id={"tm": peer},
            device_id_type=pl.DeviceIdType.MESH,
        )

    def own_in(series, j):
        return pltpu.make_async_copy(
            inputs[series].at[me * each + j], held.at[series, j, my_rows], in_recv.at[series, j, 0]
        )

    def send_out(which, j, step):
        peer = lax.rem(me + step, parts)
        return pltpu.make_async_remote_copy(
            src_ref=done.at[which, j, peer_rows(peer)],
            dst_ref=outputs[which].at[me * each + j],
            send_sem=out_send.at[which, j, step],
            recv_sem=out_recv.at[which, j, step],
            device_id={"tm": peer},
            device_id_type=pl.DeviceIdType.MESH,
        )

    def own_out(which, j):
        return pltpu.make_async_copy(
            done.at[which, j, my_rows], outputs[which].at[me * each + j], out_recv.at[which, j, 0]
        )

    tables = (
        pltpu.make_async_copy(first_in, first, table_sem.at[0]),
        pltpu.make_async_copy(second_in, second, table_sem.at[1]),
        pltpu.make_async_copy(last_in, last, table_sem.at[2]),
        pltpu.make_async_copy(turn_in, turn, table_sem.at[3]),
    )
    barrier = pltpu.get_barrier_semaphore()

    @pl.loop(1, parts)
    def _(step):
        pl.semaphore_signal(
            barrier,
            inc=1,
            device_id={"tm": lax.rem(me + step, parts)},
            device_id_type=pl.DeviceIdType.MESH,
        )

    pl.semaphore_wait(barrier, parts - 1)

    @pl.loop(0, each)
    def _(j):
        for series in range(3):

            @pl.loop(1, parts)
            def _(step):
                send_in(series, j, step).start()

            own_in(series, j).start()

    for table in tables:
        table.start()
    terms_out[...] = jnp.zeros_like(terms_out)
    for table in tables:
        table.wait()

    def forward(series, j):
        own_in(series, j).wait()

        @pl.loop(1, parts)
        def _(step):
            send_in(series, j, step).wait_recv()

        for at in range(FACTOR // TILE):
            here = pl.ds(at * TILE, TILE)
            there = pl.ds(FACTOR + at * TILE, TILE)
            part = dot3((first[0], first[1]), halves(held[series, j, :, here]))
            real_part, imag_part = part[:ROWS], part[ROWS:]
            turn_cos, turn_sin = turn[0, :, here], turn[1, :, here]
            mid_high[:, here], mid_low[:, here] = halves(real_part * turn_cos + imag_part * turn_sin)
            mid_high[:, there], mid_low[:, there] = halves(
                imag_part * turn_cos - real_part * turn_sin
            )

        @pl.loop(0, 2 * FACTOR // TILE)
        def _(at):
            here = pl.ds(pl.multiple_of(at * TILE, TILE), TILE)
            spectra[series, :, here] = dot3(
                (mid_high[...], mid_low[...]), (second[0, :, here], second[1, :, here])
            )

    def spectral(at, peak):
        rows = pl.ds(pl.multiple_of(at * 16, 16), 16)
        even, odd = pl.ds(0, FACTOR), pl.ds(FACTOR, FACTOR)
        kernel_even, kernel_odd = spectra[KERNEL, rows, even], spectra[KERNEL, rows, odd]
        sparse_even, sparse_odd = spectra[SPARSE, rows, even], spectra[SPARSE, rows, odd]
        target_even, target_odd = spectra[TARGET, rows, even], spectra[TARGET, rows, odd]
        resid_even = target_even - (kernel_even * sparse_even - kernel_odd * sparse_odd)
        resid_odd = target_odd - (kernel_even * sparse_odd + kernel_odd * sparse_even)
        grad_even = kernel_even * resid_even + kernel_odd * resid_odd
        grad_odd = kernel_even * resid_odd - kernel_odd * resid_even
        back_high[0, rows, even], back_low[0, rows, even] = halves(resid_even)
        back_high[0, rows, odd], back_low[0, rows, odd] = halves(resid_odd)
        back_high[1, rows, even], back_low[1, rows, even] = halves(grad_even)
        back_high[1, rows, odd], back_low[1, rows, odd] = halves(grad_odd)
        return jnp.maximum(peak, kernel_even * kernel_even + kernel_odd * kernel_odd)

    def inverse(which, at):
        here = pl.ds(pl.multiple_of(at * TILE, TILE), TILE)
        there = pl.ds(pl.multiple_of(FACTOR + at * TILE, TILE), TILE)
        both = (back_high[which], back_low[which])
        real_part = dot3(both, (second[0, :, here], second[1, :, here]))
        imag_part = dot3(both, (second[0, :, there], second[1, :, there]))
        turn_cos, turn_sin = turn[0, :, here], turn[1, :, here]
        turned_real = real_part * turn_cos - imag_part * turn_sin
        turned_imag = (real_part * turn_sin + imag_part * turn_cos)[:HALF]
        row = lax.broadcasted_iota(jnp.int32, (HALF, TILE), 0)
        turned_imag = jnp.where(row == 0, turned_real[HALF : HALF + 1], turned_imag)
        packed = jnp.concatenate((turned_real[:HALF], turned_imag), 0)
        return here, dot3((last[0], last[1]), halves(packed))

    @pl.loop(0, each)
    def _(j):
        for series in range(3):
            forward(series, j)
        peak = lax.fori_loop(0, ROWS // 16, spectral, jnp.zeros((16, FACTOR), jnp.float32))
        peak = jnp.max(jnp.max(peak, axis=0, keepdims=True), axis=1, keepdims=True)
        step_size = 1.0 / peak
        penalty = penalty_in[j][0:1, 0:1]
        limit = step_size * penalty

        @pl.loop(0, FACTOR // TILE)
        def _(at):
            here, residual = inverse(0, at)
            done[0, j, :, here] = residual
            terms_out[0:1, here] += jnp.sum(
                0.5 * (residual * residual) + penalty * jnp.abs(held[SPARSE, j, :, here]),
                axis=0,
                keepdims=True,
            )

        @pl.loop(1, parts)
        def _(step):
            send_out(0, j, step).start()

        own_out(0, j).start()

        @pl.loop(0, FACTOR // TILE)
        def _(at):
            here, gradient = inverse(1, at)
            moved = held[SPARSE, j, :, here] + step_size * gradient
            done[1, j, :, here] = moved - jnp.minimum(jnp.maximum(moved, -limit), limit)

        @pl.loop(1, parts)
        def _(step):
            send_out(1, j, step).start()

        own_out(1, j).start()

    @pl.loop(0, each)
    def _(j):
        for series in range(3):

            @pl.loop(1, parts)
            def _(step):
                send_in(series, j, step).wait_send()

        for which in range(2):
            own_out(which, j).wait()

            @pl.loop(1, parts)
            def _(step):
                send_out(which, j, step).wait()


def shards(target, sparse, kernel, penalty):
    parts = lax.axis_size("tm")
    me = lax.axis_index("tm")
    counters, span = sparse.shape
    each = counters // parts
    block_rows = span // FACTOR
    first, second, last, turn = make_tables()
    tiled = [x.reshape(counters, block_rows, FACTOR) for x in (kernel, sparse, target)]
    mine = lax.dynamic_slice(penalty, (me * each,), (each,))
    mine = jnp.broadcast_to(mine[:, None, None], (each, 8, 128))
    anywhere = pl.BlockSpec(memory_space=pl.ANY)
    in_vmem = pl.BlockSpec(memory_space=pltpu.VMEM)
    block = jax.ShapeDtypeStruct((counters, block_rows, FACTOR), jnp.float32)
    bf16, f32 = jnp.bfloat16, jnp.float32
    updated, residual, terms = pl.pallas_call(
        functools.partial(body, parts, each, block_rows),
        out_shape=(block, block, jax.ShapeDtypeStruct((8, FACTOR), f32)),
        in_specs=[anywhere] * 3 + [in_vmem] + [anywhere] * 4,
        out_specs=(anywhere, anywhere, in_vmem),
        scratch_shapes=[
            pltpu.VMEM((3, each, FACTOR, FACTOR), f32),
            pltpu.VMEM((3, ROWS, 2 * FACTOR), f32),
            pltpu.VMEM((ROWS, 2 * FACTOR), bf16),
            pltpu.VMEM((ROWS, 2 * FACTOR), bf16),
            pltpu.VMEM((2, ROWS, 2 * FACTOR), bf16),
            pltpu.VMEM((2, ROWS, 2 * FACTOR), bf16),
            pltpu.VMEM((2, each, FACTOR, FACTOR), f32),
            pltpu.VMEM(first.shape, bf16),
            pltpu.VMEM(second.shape, bf16),
            pltpu.VMEM(last.shape, bf16),
            pltpu.VMEM(turn.shape, f32),
            pltpu.SemaphoreType.DMA((4,)),
            pltpu.SemaphoreType.DMA((3, each, parts)),
            pltpu.SemaphoreType.DMA((3, each, parts)),
            pltpu.SemaphoreType.DMA((2, each, parts)),
            pltpu.SemaphoreType.DMA((2, each, parts)),
        ],
        compiler_params=pltpu.CompilerParams(
            collective_id=0, has_side_effects=True, vmem_limit_bytes=48 * 2**20
        ),
        cost_estimate=pl.CostEstimate(
            flops=30 * 10**9, bytes_accessed=30 * 10**6, transcendentals=0
        ),
    )(*tiled, mine, first, second, last, turn)
    total = lax.psum(jnp.sum(terms), ("tm", "ctr"))
    objective = total / (span * parts * counters * lax.axis_size("ctr"))
    return (
        updated.reshape(counters, span),
        residual.reshape(counters, span),
        objective,
    )


def solution(mesh):
    placed = (P("ctr", "tm"), P("ctr", "tm"), P("ctr", "tm"), P("ctr"))
    return jax.shard_map(
        shards,
        mesh=mesh,
        in_specs=placed,
        out_specs=(P("ctr", "tm"), P("ctr", "tm"), P()),
        check_vma=False,
    )
```

time: 811 us -> 178 us (0.22); the launches traced: 799 us -> 178 us
  matrix products: 229 us -> 0 us
  waiting for transfers between devices: 192 us -> 0 us
  local copies, waits for them, and re-layouts: 206 us -> 15.3 us
  Pallas kernels: 0 us -> 119 us
  blocking collectives: 95.6 us -> 40.3 us
  other arithmetic: 43.1 us -> 0.6 us
  starting transfers between devices: 29.1 us -> 0 us
    dot_general x12 -> x0, matrix products: 229 us -> none  [left_product(): jnp.dot(table, matrix, precision=HIGHEST, preferred_element_type=jnp.floa...]
    all_to_all x6 -> x0, waiting for transfers between devices: 192 us -> none  [the longest x1 68 us: shards(): lax.all_to_all(outgoing, 'tm', split_axis=1, concat_axis=0, tiled=True)]
    reshape x15 -> x0, local copies, waits for them, and re-layouts: 149 us -> none  [the longest x8 84 us: regroup_rows(): shaped = matrix.reshape(parts, width, groups, counters, width)]
    pallas_call x0 -> x1, Pallas kernels: none -> 119 us  [shards(): pl.pallas_call(functools.partial(body, parts, each, block_rows), out_shap...]
    pmax x1 -> x0, blocking collectives: 55.3 us -> none  [shards(): peak_power = lax.pmax(local_peak, 'tm')]
    another operation x6 -> x0, local copies, waits for them, and re-layouts: 30.4 us -> none  [shards(): jnp.stack((sparse, target, kernel), 0)]
    all_to_all x6 -> x0, starting transfers between devices: 29.1 us -> none  [the longest x1 5.17 us: shards(): lax.all_to_all(outgoing, 'tm', split_axis=1, concat_axis=0, tiled=True)]
    unnamed x12 -> x17, local copies, waits for them, and re-layouts: 0.02 us -> 14.5 us
  transfers between devices with their start and end apart: 6 -> 0, of which waited for: 5 -> 0; matrix products, arithmetic and copies ran while one was open for 15% -> 0% of each run, Pallas kernels for 0% -> 0%
where the time goes in v1:
time: 178 us
  Pallas kernels  119 us (67%)
  blocking collectives  40.3 us (23%)
  local copies, waits for them, and re-layouts  15.3 us (9%)
  between operations  2.45 us (1%)
    pallas_call x1, Pallas kernels, shards(): pl.pallas_call(functools.partial(body, parts, each, block_rows), out_shap...  119 us
    psum x1, blocking collectives, shards(): total = lax.psum(jnp.sum(terms), ('tm', 'ctr'))  40.3 us
    unnamed x17, local copies, waits for them, and re-layouts  14.5 us

profile of v1, /device:TPU:0, one launch (start us, length us, event | category | flops | bytes accessed | tf_op | source)
XLA Modules:
  0.0 177.5 jit_solution(2464251402423350936)
XLA Ops:
  0.6 0.7 dynamic_slice.3
  1.4 0.1 broadcast_in_dim.2.penalty_in
  1.4 0.0 copy-start.3
  1.4 4.3 %copy.13 = f32[2,8,64,512]{3,2,1,0:T(8,128)} copy(f32[2,8,64,512]{3,1,2,0:T(8,128)} %bitcast.11) | data formatting | bytes 4194304
  5.7 0.0 copy-done.3
  5.7 0.0 copy-start.4
  5.7 2.5 %copy.12 = f32[2,8,64,512]{3,2,1,0:T(8,128)} copy(f32[2,8,64,512]{3,1,2,0:T(8,128)S(1)} %bitcast.12) | data formatting | bytes 4194304
  8.3 0.0 copy-done.4
  8.3 0.0 copy-start
  8.3 0.0 copy-start.1
  8.3 0.0 copy-start.2
  8.3 2.5 %copy.11 = f32[2,8,64,512]{3,2,1,0:T(8,128)} copy(f32[2,8,64,512]{3,1,2,0:T(8,128)S(1)} %bitcast.13) | data formatting | bytes 4194304
  10.8 0.0 copy-done
  10.8 0.0 copy-done.1
  10.8 0.0 copy-done.2
  10.8 118.9 %shard_map.103 = (f32[16,64,512]{2,1,0:T(8,128)S(1)}, f32[16,64,512]{2,1,0:T(8,128)}, f32[8,512]{1,0:T(8,128)S(1)}) custom-call(f32[16,64,512]{2,1,0:T(8,128)} %bitcast.17, f32[16,64,512]{2,1,0:T(8,128)} %bitcast.16, f32[16,64,512]{2,1,0:T(8,128)} %bitcast.15, f32[2,8,128]{2,1,0:T(8,128)S(1)} %broadcast_in_dim.2.penalty_in, ...), custom_call_target="tpu_custom_call" | custom-call | flops 30000001024 | bytes 30000000 | tf_op jit(solution)/shard_map/pallas_call | solution.py:291
  129.8 0.6 reduce_sum.9
  130.4 40.3 %psum.7 = f32[]{:T(128)} all-reduce(f32[]{:T(128)} %reduce_sum.9), channel_id=1, replica_groups=mesh['tm'=8,'ctr'=4] {'tm','ctr'}, use_global_device_ids=true, to_apply=%region_1.0 | all-reduce | flops 1 | bytes 8 | tf_op jit(solution)/shard_map/psum | solution.py:321
  171.3 0.0 copy-start.5
  171.3 2.5 %copy.14 = f32[2,8,64,512]{3,1,2,0:T(8,128)} copy(f32[2,8,64,512]{3,2,1,0:T(8,128)S(1)} %bitcast.10) | data formatting | bytes 4194304
  173.9 0.0 copy-done.5
  173.9 2.5 %copy.15 = f32[2,8,64,512]{3,1,2,0:T(8,128)} copy(f32[2,8,64,512]{3,2,1,0:T(8,128)S(1)} %bitcast.14) | data formatting | bytes 4194304
Async XLA Ops:
  1.4 4.3 %copy-start.3 = (f32[16,32768]{1,0:T(8,128)S(1)}, f32[16,32768]{1,0:T(8,128)}, u32[]{:S(2)}) copy-start(f32[16,32768]{1,0:T(8,128)} %param.9) | copy-start | bytes 6291460
  5.7 2.5 %copy-start.4 = (f32[16,32768]{1,0:T(8,128)S(1)}, f32[16,32768]{1,0:T(8,128)}, u32[]{:S(2)}) copy-start(f32[16,32768]{1,0:T(8,128)} %param.10) | copy-start | bytes 6291460
  8.3 2.5 %copy-start = (f32[2,272,512]{2,1,0:T(8,128)S(1)}, f32[2,272,512]{2,1,0:T(8,128)}, u32[]{:S(2)}) copy-start(f32[2,272,512]{2,1,0:T(8,128)} %constant.28.clone.turn_in) | copy-start | bytes 3342340
  8.3 2.5 %copy-start.1 = (bf16[2,544,512]{2,1,0:T(8,128)(2,1)S(1)}, bf16[2,544,512]{2,1,0:T(8,128)(2,1)}, u32[]{:S(2)}) copy-start(bf16[2,544,512]{2,1,0:T(8,128)(2,1)} %constant.25.clone.first_in) | copy-start | bytes 3342340
  8.3 2.5 %copy-start.2 = (bf16[2,512,512]{2,1,0:T(8,128)(2,1)S(1)}, bf16[2,512,512]{2,1,0:T(8,128)(2,1)}, u32[]{:S(2)}) copy-start(bf16[2,512,512]{2,1,0:T(8,128)(2,1)} %constant.27.clone.last_in) | copy-start | bytes 3145732
  171.3 2.5 %copy-start.5 = (f32[16,64,512]{2,1,0:T(8,128)S(1)}, f32[16,64,512]{2,1,0:T(8,128)}, u32[]{:S(2)}) copy-start(f32[16,64,512]{2,1,0:T(8,128)} %get-tuple-element.7) | copy-start | bytes 6291460

commit v2 on v1

--- a/solution.py
+++ b/solution.py
@@ -60,8 +60,10 @@
 
 def body(
     parts,
+    groups,
     each,
     block_rows,
+    scale,
     kernel_in,
     sparse_in,
     target_in,
@@ -72,7 +74,10 @@
     turn_in,
     updated_out,
     residual_out,
-    terms_out,
+    objective_out,
+    terms,
+    by_group,
+    by_part,
     held,
     spectra,
     mid_high,
@@ -89,19 +94,27 @@
     in_recv,
     out_send,
     out_recv,
+    group_send,
+    group_recv,
+    part_send,
+    part_recv,
 ):
     me = lax.axis_index("tm")
+    group = lax.axis_index("ctr")
     my_rows = pl.ds(pl.multiple_of(me * block_rows, block_rows), block_rows)
     inputs = (kernel_in, sparse_in, target_in)
     outputs = (residual_out, updated_out)
 
+    def row_of(ref, counter):
+        return ref.at[lax.div(counter, 8), :, lax.rem(counter, 8)]
+
     def peer_rows(peer):
         return pl.ds(pl.multiple_of(peer * block_rows, block_rows), block_rows)
 
     def send_in(series, j, step):
         peer = lax.rem(me + step, parts)
         return pltpu.make_async_remote_copy(
-            src_ref=inputs[series].at[peer * each + j],
+            src_ref=row_of(inputs[series], peer * each + j),
             dst_ref=held.at[series, j, my_rows],
             send_sem=in_send.at[series, j, step],
             recv_sem=in_recv.at[series, j, step],
@@ -111,14 +124,14 @@
 
     def own_in(series, j):
         return pltpu.make_async_copy(
-            inputs[series].at[me * each + j], held.at[series, j, my_rows], in_recv.at[series, j, 0]
+            row_of(inputs[series], me * each + j), held.at[series, j, my_rows], in_recv.at[series, j, 0]
         )
 
     def send_out(which, j, step):
         peer = lax.rem(me + step, parts)
         return pltpu.make_async_remote_copy(
             src_ref=done.at[which, j, peer_rows(peer)],
-            dst_ref=outputs[which].at[me * each + j],
+            dst_ref=row_of(outputs[which], me * each + j),
             send_sem=out_send.at[which, j, step],
             recv_sem=out_recv.at[which, j, step],
             device_id={"tm": peer},
@@ -127,7 +140,29 @@
 
     def own_out(which, j):
         return pltpu.make_async_copy(
-            done.at[which, j, my_rows], outputs[which].at[me * each + j], out_recv.at[which, j, 0]
+            done.at[which, j, my_rows],
+            row_of(outputs[which], me * each + j),
+            out_recv.at[which, j, 0],
+        )
+
+    def send_group(step):
+        return pltpu.make_async_remote_copy(
+            src_ref=by_group.at[group],
+            dst_ref=by_group.at[group],
+            send_sem=group_send.at[step],
+            recv_sem=group_recv.at[step],
+            device_id={"ctr": lax.rem(group + step, groups)},
+            device_id_type=pl.DeviceIdType.MESH,
+        )
+
+    def send_part(step):
+        return pltpu.make_async_remote_copy(
+            src_ref=by_part.at[me],
+            dst_ref=by_part.at[me],
+            send_sem=part_send.at[step],
+            recv_sem=part_recv.at[step],
+            device_id={"tm": lax.rem(me + step, parts)},
+            device_id_type=pl.DeviceIdType.MESH,
         )
 
     tables = (
@@ -147,7 +182,16 @@
             device_id_type=pl.DeviceIdType.MESH,
         )
 
-    pl.semaphore_wait(barrier, parts - 1)
+    @pl.loop(1, groups)
+    def _(step):
+        pl.semaphore_signal(
+            barrier,
+            inc=1,
+            device_id={"ctr": lax.rem(group + step, groups)},
+            device_id_type=pl.DeviceIdType.MESH,
+        )
+
+    pl.semaphore_wait(barrier, parts + groups - 2)
 
     @pl.loop(0, each)
     def _(j):
@@ -161,9 +205,16 @@
 
     for table in tables:
         table.start()
-    terms_out[...] = jnp.zeros_like(terms_out)
+    terms[...] = jnp.zeros_like(terms)
     for table in tables:
         table.wait()
+
+    def send_updated(j):
+        @pl.loop(1, parts)
+        def _(step):
+            send_out(1, j, step).start()
+
+        own_out(1, j).start()
 
     def forward(series, j):
         own_in(series, j).wait()
@@ -171,6 +222,12 @@
         @pl.loop(1, parts)
         def _(step):
             send_in(series, j, step).wait_recv()
+
+        if series == 2:
+
+            @pl.when(j > 0)
+            def _():
+                send_updated(j - 1)
 
         for at in range(FACTOR // TILE):
             here = pl.ds(at * TILE, TILE)
@@ -227,14 +284,14 @@
         peak = lax.fori_loop(0, ROWS // 16, spectral, jnp.zeros((16, FACTOR), jnp.float32))
         peak = jnp.max(jnp.max(peak, axis=0, keepdims=True), axis=1, keepdims=True)
         step_size = 1.0 / peak
-        penalty = penalty_in[j][0:1, 0:1]
+        penalty = penalty_in[me * each + j]
         limit = step_size * penalty
 
         @pl.loop(0, FACTOR // TILE)
         def _(at):
             here, residual = inverse(0, at)
             done[0, j, :, here] = residual
-            terms_out[0:1, here] += jnp.sum(
+            terms[0:1, here] += jnp.sum(
                 0.5 * (residual * residual) + penalty * jnp.abs(held[SPARSE, j, :, here]),
                 axis=0,
                 keepdims=True,
@@ -245,6 +302,16 @@
             send_out(0, j, step).start()
 
         own_out(0, j).start()
+
+        @pl.when(j == each - 1)
+        def _():
+            total = jnp.sum(terms[...], axis=0, keepdims=True)
+            total = jnp.sum(total, axis=1, keepdims=True)
+            by_group[group] = jnp.broadcast_to(total, (8, 128))
+
+            @pl.loop(1, groups)
+            def _(step):
+                send_group(step).start()
 
         @pl.loop(0, FACTOR // TILE)
         def _(at):
@@ -252,11 +319,37 @@
             moved = held[SPARSE, j, :, here] + step_size * gradient
             done[1, j, :, here] = moved - jnp.minimum(jnp.maximum(moved, -limit), limit)
 
-        @pl.loop(1, parts)
-        def _(step):
-            send_out(1, j, step).start()
-
-        own_out(1, j).start()
+    @pl.loop(1, groups)
+    def _(step):
+        send_group(step).wait_recv()
+
+    total = by_group[0]
+    for other in range(1, groups):
+        total = total + by_group[other]
+    by_part[me] = total
+
+    @pl.loop(1, parts)
+    def _(step):
+        send_part(step).start()
+
+    send_updated(each - 1)
+
+    @pl.loop(1, parts)
+    def _(step):
+        send_part(step).wait_recv()
+
+    total = by_part[0]
+    for other in range(1, parts):
+        total = total + by_part[other]
+    objective_out[...] = total * scale
+
+    @pl.loop(1, groups)
+    def _(step):
+        send_group(step).wait_send()
+
+    @pl.loop(1, parts)
+    def _(step):
+        send_part(step).wait_send()
 
     @pl.loop(0, each)
     def _(j):
@@ -276,24 +369,26 @@
 
 def shards(target, sparse, kernel, penalty):
     parts = lax.axis_size("tm")
-    me = lax.axis_index("tm")
+    groups = lax.axis_size("ctr")
     counters, span = sparse.shape
     each = counters // parts
     block_rows = span // FACTOR
     first, second, last, turn = make_tables()
-    tiled = [x.reshape(counters, block_rows, FACTOR) for x in (kernel, sparse, target)]
-    mine = lax.dynamic_slice(penalty, (me * each,), (each,))
-    mine = jnp.broadcast_to(mine[:, None, None], (each, 8, 128))
+    tiled = [x.reshape(counters // 8, 8, block_rows, FACTOR).transpose(0, 2, 1, 3) for x in (kernel, sparse, target)]
+    scale = 1.0 / (span * parts * counters * groups)
     anywhere = pl.BlockSpec(memory_space=pl.ANY)
     in_vmem = pl.BlockSpec(memory_space=pltpu.VMEM)
-    block = jax.ShapeDtypeStruct((counters, block_rows, FACTOR), jnp.float32)
+    block = jax.ShapeDtypeStruct((counters // 8, block_rows, 8, FACTOR), jnp.float32)
     bf16, f32 = jnp.bfloat16, jnp.float32
-    updated, residual, terms = pl.pallas_call(
-        functools.partial(body, parts, each, block_rows),
-        out_shape=(block, block, jax.ShapeDtypeStruct((8, FACTOR), f32)),
-        in_specs=[anywhere] * 3 + [in_vmem] + [anywhere] * 4,
+    updated, residual, objective = pl.pallas_call(
+        functools.partial(body, parts, groups, each, block_rows, scale),
+        out_shape=(block, block, jax.ShapeDtypeStruct((8, 128), f32)),
+        in_specs=[anywhere] * 3 + [pl.BlockSpec(memory_space=pltpu.SMEM)] + [anywhere] * 4,
         out_specs=(anywhere, anywhere, in_vmem),
         scratch_shapes=[
+            pltpu.VMEM((8, FACTOR), f32),
+            pltpu.VMEM((groups, 8, 128), f32),
+            pltpu.VMEM((parts, 8, 128), f32),
             pltpu.VMEM((3, each, FACTOR, FACTOR), f32),
             pltpu.VMEM((3, ROWS, 2 * FACTOR), f32),
             pltpu.VMEM((ROWS, 2 * FACTOR), bf16),
@@ -310,20 +405,22 @@
             pltpu.SemaphoreType.DMA((3, each, parts)),
             pltpu.SemaphoreType.DMA((2, each, parts)),
             pltpu.SemaphoreType.DMA((2, each, parts)),
+            pltpu.SemaphoreType.DMA((groups,)),
+            pltpu.SemaphoreType.DMA((groups,)),
+            pltpu.SemaphoreType.DMA((parts,)),
+            pltpu.SemaphoreType.DMA((parts,)),
         ],
         compiler_params=pltpu.CompilerParams(
-            collective_id=0, has_side_effects=True, vmem_limit_bytes=48 * 2**20
+            collective_id=0, has_side_effects=True, vmem_limit_bytes=60 * 2**20
         ),
         cost_estimate=pl.CostEstimate(
             flops=30 * 10**9, bytes_accessed=30 * 10**6, transcendentals=0
         ),
-    )(*tiled, mine, first, second, last, turn)
-    total = lax.psum(jnp.sum(terms), ("tm", "ctr"))
-    objective = total / (span * parts * counters * lax.axis_size("ctr"))
+    )(*tiled, penalty, first, second, last, turn)
     return (
-        updated.reshape(counters, span),
-        residual.reshape(counters, span),
-        objective,
+        updated.transpose(0, 2, 1, 3).reshape(counters, span),
+        residual.transpose(0, 2, 1, 3).reshape(counters, span),
+        objective[0, 0],
     )
 
 

time: 178 us -> 129 us (0.72)
  blocking collectives: 40.3 us -> 0 us
  local copies, waits for them, and re-layouts: 15.3 us -> 5.7 us
  Pallas kernels: 119 us -> 122 us
  between operations: 2.45 us -> 0.64 us
    psum x1 -> x0, blocking collectives: 40.3 us -> none  [shards(): total = lax.psum(jnp.sum(terms), ('tm', 'ctr'))]
    unnamed x17 -> x4, local copies, waits for them, and re-layouts: 14.5 us -> 4.52 us
    pallas_call x1, Pallas kernels: 119 us -> 122 us  [shards(): pl.pallas_call(functools.partial(body, parts, groups, each, block_rows, s...]
where the time goes in v2:
time: 129 us; the launch traced here: 128 us
  Pallas kernels  122 us (95%)
  local copies, waits for them, and re-layouts  5.7 us (4%)
    pallas_call x1, Pallas kernels, shards(): pl.pallas_call(functools.partial(body, parts, groups, each, block_rows, s...  122 us
    unnamed x4, local copies, waits for them, and re-layouts  4.52 us

profile of v2, /device:TPU:0, one launch (start us, length us, event | category | flops | bytes accessed | tf_op | source)
XLA Modules:
  0.0 128.1 jit_solution(708595998407695220)
XLA Ops:
  0.6 121.8 %shard_map.103 = (f32[2,64,8,512]{3,2,1,0:T(8,128)}, f32[2,64,8,512]{3,2,1,0:T(8,128)}, f32[8,128]{1,0:T(8,128)}) custom-call(f32[2,64,8,512]{3,2,1,0:T(8,128)} %bitcast.18, f32[2,64,8,512]{3,2,1,0:T(8,128)} %bitcast.19, f32[2,64,8,512]{3,2,1,0:T(8,128)} %bitcast.20, f32[16]{0:T(128)} %penalty_in.1, bf16[2,544,512]{2,1,0:T(8,128)(2,1)} %constant.8.clone.first_in, ...), custom_call_target="tpu_custom_call" | custom-call | flops 30000001024 | bytes 30000000 | tf_op jit(solution)/shard_map/pallas_call | solution.py:383
  122.4 1.2 slice.3
  123.6 0.0 copy-start
  123.6 3.2 %copy.13 = f32[16,32768]{1,0:T(8,128)} copy(f32[16,32768]{1,0:T(8,128)} %bitcast.17) | data formatting | bytes 4194304
  126.8 0.0 copy-done
  126.8 1.3 %copy.14 = f32[16,32768]{1,0:T(8,128)} copy(f32[16,32768]{1,0:T(8,128)S(1)} %bitcast.16) | data formatting | bytes 4194304
Async XLA Ops:
  123.6 3.2 %copy-start = (f32[2,64,8,512]{3,2,1,0:T(8,128)S(1)}, f32[2,64,8,512]{3,2,1,0:T(8,128)}, u32[]{:S(2)}) copy-start(f32[2,64,8,512]{3,2,1,0:T(8,128)} %get-tuple-element.7) | copy-start | bytes 6291460
